TPU v7x, 256 devices: a whole 4x4x8 slice. The times are simulated.
256 devices in a mesh: px: 4 (over z_hi), py: 8 (over y, core), mz: 8 (over z_lo, x).
Axes of the slice: x: 4, y: 4, z: 8 (z_hi: 4, z_lo: 2; z = z_hi * 2 + z_lo), core: 2. Of those that a mesh axis runs over, the one named last changes fastest.
Arguments:
- tensor: float32 [512, 1024, 1024], P('px', 'py', 'mz'), may hold values from 0 to 1573632, as said below
- factor_a: float32 [512, 256], P('px'), may hold values from 0 to 1
- factor_b: float32 [1024, 256], P('py'), may hold values from 0 to 1
- factor_c: float32 [1024, 256], P('mz'), may hold values from 0 to 1
Outputs:
- new_a: float32 [512, 256], P('px')
- new_b: float32 [1024, 256], P('py')
- new_c: float32 [1024, 256], P('mz')
Inputs may be any that keep to these rules, and one draw needn't show every extreme that they name: `tensor`: nonnegative intensities.
All inputs are finite; a program needn't handle non-finite values.
Results may differ from a plain program's by a relative error of at most 0.00015.
Values sent between devices are 32-bit elements; how exact they have to be, the bound alone decides.
No kernel may reach another device: no remote copies, remote signals or barrier semaphores. Data moves between devices by JAX's collectives and lax.ppermute only.
A program may use at most 128 MiB of HBM per device.

v0:
```python
import jax
import jax.numpy as jnp
from jax import lax
from jax.sharding import PartitionSpec as P

PASSES = 2


exact_mode = lax.Precision.HIGHEST


def gram_of(factor):
    return jnp.dot(factor.T, factor, precision=exact_mode, preferred_element_type=jnp.float32)


def full_passes(factor, mttkrp, gram_mix):
    scale_cols = jnp.sum(gram_mix, axis=0) + 1.0
    for sweep_pass in range(PASSES):
        product = jnp.dot(
            factor, gram_mix, precision=exact_mode, preferred_element_type=jnp.float32
        )
        factor = jnp.maximum(factor + (mttkrp - product) / scale_cols, 0.0)
    return factor


def per_device(tensor, factor_a, factor_b, factor_c):
    rows_x, rows_y, rows_z = tensor.shape
    gram_b = lax.psum(gram_of(factor_b), "py")
    gram_c = lax.psum(gram_of(factor_c), "mz")
    partial_c = jnp.dot(
        tensor.reshape(rows_x * rows_y, rows_z),
        factor_c,
        precision=exact_mode,
        preferred_element_type=jnp.float32,
    )
    local_a = jnp.einsum(
        "ijr,jr->ir",
        partial_c.reshape(rows_x, rows_y, -1),
        factor_b,
        precision=exact_mode,
        preferred_element_type=jnp.float32,
    )
    mttkrp_a = lax.psum(local_a, ("py", "mz"))
    new_a = full_passes(factor_a, mttkrp_a, gram_b * gram_c)
    gram_a = lax.psum(gram_of(new_a), "px")
    partial_a = lax.dot_general(
        new_a,
        tensor.reshape(rows_x, rows_y * rows_z),
        (((0,), (0,)), ((), ())),
        precision=exact_mode,
        preferred_element_type=jnp.float32,
    )
    partial_a = partial_a.reshape(-1, rows_y, rows_z)
    local_b = jnp.einsum(
        "rjk,kr->jr", partial_a, factor_c, precision=exact_mode, preferred_element_type=jnp.float32
    )
    mttkrp_b = lax.psum(local_b, ("px", "mz"))
    new_b = full_passes(factor_b, mttkrp_b, gram_a * gram_c)
    gram_bn = lax.psum(gram_of(new_b), "py")
    local_c = jnp.einsum(
        "rjk,jr->kr", partial_a, new_b, precision=exact_mode, preferred_element_type=jnp.float32
    )
    mttkrp_c = lax.psum(local_c, ("px", "py"))
    new_c = full_passes(factor_c, mttkrp_c, gram_a * gram_bn)
    return (new_a, new_b, new_c)


def solution(mesh):
    in_specs = (P("px", "py", "mz"), P("px", None), P("py", None), P("mz", None))
    out_specs = (P("px", None), P("py", None), P("mz", None))
    return jax.shard_map(
        per_device, mesh=mesh, in_specs=in_specs, out_specs=out_specs, check_vma=False
    )
```

profile of v0, /device:TPU:1, one launch (start us, length us, event | category | flops | bytes accessed | tf_op | source)
XLA Modules:
  0.0 1200.7 jit_solution(6588989719215688766)
XLA Ops:
  7.2 0.0 all-reduce.10.cloned.1.call-start
  7.2 2.1 fusion.31
  9.3 0.0 all-reduce.10.cloned.1.call-update
  9.3 0.0 all-reduce.12.cloned.1.call-start
  9.4 2.1 fusion.32
  11.5 0.0 all-reduce.12.cloned.1.call-update
  11.5 0.0 all-reduce.8.cloned.1.call-start
  11.6 15.5 %multiply_reduce_fusion = f32[256,128]{0,1:T(8,128)S(1)} fusion(f32[128,128,128]{2,1,0:T(8,128)} %param.4, f32[256,128]{0,1:T(8,128)} %bitcast.87, f32[128,256]{1,0:T(8,128)} %param.7), kind=kOutput, calls=%fused_computation | convolution fusion | flops 6450806784 | bytes 8781824 | tf_op jit(solution)/shard_map/dot_general | solution.py:30
  27.0 0.8 copy.23
  27.8 0.0 all-reduce.8.cloned.1.call-update
  27.8 0.3 all-reduce.16.cloned.1.call-start
  28.2 1.0 copy.10
  29.2 1.0 copy.12
  30.2 1.0 copy.7
  31.2 13.2 %copy.39 = f32[16,8,128,128]{3,1,2,0:T(8,128)} copy(f32[16,8,128,128]{3,2,1,0:T(8,128)} %bitcast.83) | data formatting | bytes 16777216
  44.4 9.0 copy.9
  53.4 0.1 copy.26
  53.5 23.6 %all-reduce.10.cloned.1.call-done = f32[256,256]{1,0:T(8,128)} async-done(((f32[256,256]{1,0:T(8,128)}), f32[256,256]{1,0:T(8,128)}) %all-reduce.10.cloned.1.call-update) | async-done | bytes 262160 | tf_op jit(solution)/shard_map/psum | solution.py:28
  77.1 78.2 %all-reduce.12.cloned.1.call-done = f32[256,256]{1,0:T(8,128)} async-done(((f32[256,256]{1,0:T(8,128)}), f32[256,256]{1,0:T(8,128)}) %all-reduce.12.cloned.1.call-update) | async-done | bytes 262160 | tf_op jit(solution)/shard_map/psum | solution.py:29
  155.3 1.1 fusion.30
  156.4 493.1 %all-reduce.8.cloned.1.call-done = f32[128,256]{0,1:T(8,128)} async-done(((f32[128,256]{0,1:T(8,128)}), f32[128,256]{0,1:T(8,128)}) %all-reduce.8.cloned.1.call-update) | async-done | bytes 131088 | tf_op jit(solution)/shard_map/psum | solution.py:43
  649.5 1.5 fusion.24
  651.0 1.5 fusion.20
  652.5 1.1 fusion.33
  653.6 0.0 all-reduce.16.cloned.1.call-update
  653.6 0.6 all-reduce.14.cloned.1.call-start
  654.2 16.4 %fusion.25 = f32[256,128,128]{2,0,1:T(8,128)S(1)} fusion(f32[128,128,128]{2,1,0:T(8,128)} %bitcast.84, f32[128,256]{0,1:T(8,128)S(1)} %fusion.20), kind=kOutput, calls=%fused_computation.33 | convolution fusion | flops 6442450944 | bytes 25296896 | tf_op jit(solution)/shard_map/dot_general | solution.py:46
  670.6 5.7 copy-done
  676.3 40.3 %fusion.2 = f32[256,1,128]{2,1,0:T(1,128)} fusion(f32[128,256,1]{0,2,1:T(1,128)S(1)} %copy.26, f32[256,128,128]{2,0,1:T(8,128)S(1)} %fusion.25), kind=kOutput, calls=%fused_computation.3 | convolution fusion | flops 50331648 | bytes 17039360 | tf_op jit(solution)/shard_map/rjk,kr->jr/dot_general | solution.py:54
  716.6 0.8 copy.14
  717.4 0.0 all-reduce.14.cloned.1.call-update
  717.4 0.3 all-reduce.20.cloned.1.call-start
  717.6 0.0 all-reduce.16.cloned.1.call-done
  717.7 1.0 fusion.29
  718.7 135.7 %all-reduce.14.cloned.1.call-done = f32[128,256]{0,1:T(8,128)} async-done(((f32[128,256]{0,1:T(8,128)}), f32[128,256]{0,1:T(8,128)}) %all-reduce.14.cloned.1.call-update) | async-done | bytes 131088 | tf_op jit(solution)/shard_map/psum | solution.py:57
  854.4 1.5 fusion.17
  855.9 1.5 fusion.13
  857.4 1.1 fusion.34
  858.5 0.0 all-reduce.20.cloned.1.call-update
  858.5 0.0 all-reduce.18.cloned.1.call-start
  858.5 27.6 %fusion = f32[256,1,128]{2,1,0:T(1,128)} fusion(f32[128,256,1]{0,2,1:T(1,128)S(1)} %bitcast.88, f32[256,128,128]{2,0,1:T(8,128)} %copy-done), kind=kOutput, calls=%fused_computation.1 | convolution fusion | flops 50331648 | bytes 17039360 | tf_op jit(solution)/shard_map/rjk,jr->kr/dot_general | solution.py:60
  886.1 0.8 copy.15
  886.9 36.8 %all-reduce.20.cloned.1.call-done = f32[256,256]{1,0:T(8,128)} async-done(((f32[256,256]{1,0:T(8,128)}), f32[256,256]{1,0:T(8,128)}) %all-reduce.20.cloned.1.call-update) | async-done | bytes 262160 | tf_op jit(solution)/shard_map/psum | solution.py:59
  923.7 1.0 fusion.28
  924.7 265.1 %all-reduce.18.cloned.1.call-done = f32[128,256]{0,1:T(8,128)} async-done(((f32[128,256]{0,1:T(8,128)}), f32[128,256]{0,1:T(8,128)}) %all-reduce.18.cloned.1.call-update) | async-done | bytes 131088 | tf_op jit(solution)/shard_map/psum | solution.py:63
  1189.8 1.5 fusion.10
  1191.3 1.5 fusion.6
  1192.8 0.8 copy.16
  (15 shorter events, 0.1 us)
Async XLA Ops:
  7.2 69.9 %all-reduce.10.cloned.1.call-start = ((), (), s32[]{:S(2)}) async-start(), calls=%async_computation.1 | async-start | bytes 524288 | tf_op jit(solution)/shard_map/psum | solution.py:28
  9.3 146.0 %all-reduce.12.cloned.1.call-start = ((), (), s32[]{:S(2)}) async-start(), calls=%async_computation.2 | async-start | bytes 524288 | tf_op jit(solution)/shard_map/psum | solution.py:29
  11.5 638.0 %all-reduce.8.cloned.1.call-start = ((), (), s32[]{:S(2)}) async-start(), calls=%async_computation | async-start | bytes 262144 | tf_op jit(solution)/shard_map/psum | solution.py:43
  27.8 689.8 %all-reduce.16.cloned.1.call-start = ((), (), s32[]{:S(2)}) async-start(), calls=%async_computation.4 | async-start | bytes 524288 | tf_op jit(solution)/shard_map/psum | solution.py:45
  31.2 22.2 %copy-start.1 = (f32[128,256]{1,0:T(8,128)S(1)}, f32[128,256]{1,0:T(8,128)}, u32[]{:S(2)}) copy-start(f32[128,256]{1,0:T(8,128)} %param.7) | copy-start | bytes 393220
  31.2 618.3 %copy-start.5 = (f32[128,256]{1,0:T(8,128)S(1)}, f32[128,256]{1,0:T(8,128)}, u32[]{:S(2)}) copy-start(f32[128,256]{1,0:T(8,128)} %param.5) | copy-start | bytes 393220
  653.6 200.8 %all-reduce.14.cloned.1.call-start = ((), (), s32[]{:S(2)}) async-start(), calls=%async_computation.3 | async-start | bytes 262144 | tf_op jit(solution)/shard_map/psum | solution.py:57
  670.6 5.7 copy-start
  676.3 41.4 %copy-start.3 = (f32[256,256]{1,0:T(8,128)S(1)}, f32[256,256]{1,0:T(8,128)}, u32[]{:S(2)}) copy-start(f32[256,256]{1,0:T(8,128)} %all-reduce.12.cloned.1.call-done) | copy-start | bytes 786436
  676.3 178.1 %copy-start.2 = (f32[128,256]{1,0:T(8,128)S(1)}, f32[128,256]{1,0:T(8,128)}, u32[]{:S(2)}) copy-start(f32[128,256]{1,0:T(8,128)} %param.6) | copy-start | bytes 393220
  717.4 206.3 %all-reduce.20.cloned.1.call-start = ((), (), s32[]{:S(2)}) async-start(), calls=%async_computation.6 | async-start | bytes 524288 | tf_op jit(solution)/shard_map/psum | solution.py:59
  857.4 66.3 %copy-start.4 = (f32[256,256]{1,0:T(8,128)S(1)}, f32[256,256]{1,0:T(8,128)}, u32[]{:S(2)}) copy-start(f32[256,256]{1,0:T(8,128)} %all-reduce.16.cloned.1.call-done) | copy-start | bytes 786436
  858.5 331.3 %all-reduce.18.cloned.1.call-start = ((), (), s32[]{:S(2)}) async-start(), calls=%async_computation.5 | async-start | bytes 262144 | tf_op jit(solution)/shard_map/psum | solution.py:63
Sparse Core Ops, SparseCore 0:
  10.3 66.7 all-reduce.9
  79.9 75.3 all-reduce.11
  158.5 490.9 all-reduce.7
  653.7 48.8 all-reduce.15
  717.5 136.8 all-reduce.13
  858.6 65.0 all-reduce.19
  926.9 262.9 all-reduce.17
where the time goes:
time: 1210 us; the launch traced here: 1200 us
  waiting for transfers between devices  1030 us (85%)
  matrix products  115 us (10%)
  local copies, waits for them, and re-layouts  34 us (3%)
  between operations  14.5 us (1%)
    psum x1, waiting for transfers between devices, per_device(): mttkrp_a = lax.psum(local_a, ('py', 'mz'))  493 us
    psum x1, waiting for transfers between devices, per_device(): mttkrp_c = lax.psum(local_c, ('px', 'py'))  265 us
    psum x1, waiting for transfers between devices, per_device(): mttkrp_b = lax.psum(local_b, ('px', 'mz'))  136 us
    psum x1, waiting for transfers between devices, per_device(): gram_c = lax.psum(gram_of(factor_c), 'mz')  78.2 us
    dot_general x1, matrix products, per_device(): jnp.einsum('rjk,kr->jr', partial_a, factor_c, precision=exact_mode, prefe...  40.3 us
    psum x1, waiting for transfers between devices, per_device(): gram_bn = lax.psum(gram_of(new_b), 'py')  36.8 us
    dot_general x1, matrix products, per_device(): jnp.einsum('rjk,jr->kr', partial_a, new_b, precision=exact_mode, preferre...  27.6 us
    unnamed x20, local copies, waits for them, and re-layouts  24.3 us
  transfers between devices with their start and end apart: 7, of which 6 were waited for; matrix products, arithmetic and copies ran while one was open for 11% of the time, Pallas kernels for 0%

commit v1 on v0

v1 whole, which is shorter than its diff:
```python
import functools

import jax
import jax.numpy as jnp
from jax import lax
from jax.experimental import pallas as pl
from jax.experimental.pallas import tpu as pltpu
from jax.sharding import PartitionSpec as P

PASSES = 2
F32 = jnp.float32
BF16 = jnp.bfloat16
EXACT = lax.Precision.HIGHEST
ROWS = 128
RANK = 256
CHUNKS = 8
SUB = 16


def split(x):
    hi = x.astype(BF16)
    return hi, (x - hi.astype(F32)).astype(BF16)


def stream(x):
    hi, lo = split(x)
    return jnp.concatenate([hi, lo, hi], axis=1)


def weights(x):
    hi, lo = split(x)
    return jnp.concatenate([hi, hi, lo], axis=0)


def gram_of(factor):
    return lax.dot_general(
        factor, factor, (((0,), (0,)), ((), ())), precision=EXACT, preferred_element_type=F32
    )


def updated(factor, mttkrp, mix):
    scale = jnp.sum(mix, axis=0, keepdims=True) + 1.0
    for _ in range(PASSES):
        product = jnp.dot(factor, mix, precision=EXACT, preferred_element_type=F32)
        factor = jnp.maximum(factor + (mttkrp - product) / scale, 0.0)
    return factor


def put_mttkrp(buf, value):
    buf[0:128, :] = value[:, 0:128]
    buf[128:256, :] = value[:, 128:256]


def get_mttkrp(buf):
    return jnp.concatenate([buf[0:128, :], buf[128:256, :]], axis=1)


def put_half(buf, at, gram):
    buf[at : at + 128, :] = gram[0:128, 0:128]
    buf[at + 128 : at + 256, :] = gram[0:128, 128:256]
    buf[at + 256 : at + 384, :] = gram[128:256, 128:256]


def get_half(buf, at):
    corner = buf[at + 128 : at + 256, :]
    top = jnp.concatenate([buf[at : at + 128, :], corner], axis=1)
    low = jnp.concatenate([corner.T, buf[at + 256 : at + 384, :]], axis=1)
    return jnp.concatenate([top, low], axis=0)


def put_gram(buf, gram):
    buf[256:512, :] = gram[:, 0:128]
    buf[512:768, :] = gram[:, 128:256]


def get_gram(buf):
    return jnp.concatenate([buf[256:512, :], buf[512:768, :]], axis=1)


def fetch(tensor, held, sems):
    step = ROWS // CHUNKS
    copies = []
    for c in range(CHUNKS):
        part = pl.ds(c * step, step)
        copies.append(pltpu.make_async_copy(tensor.at[part], held.at[part], sems.at[c]))
    for copy in copies:
        copy.start()
    return copies


def first_kernel(inv_b, inv_c, tensor, fb, fc, out, held, sems):
    copies = fetch(tensor, held, sems)
    b, c = fb[...], fc[...]
    put_half(out, 256, gram_of(b) * inv_b)
    put_half(out, 640, gram_of(c) * inv_c)
    wide = weights(c)
    for n in range(ROWS // SUB):
        if n * SUB % (ROWS // CHUNKS) == 0:
            copies[n * SUB // (ROWS // CHUNKS)].wait()
        block = held[n * SUB : (n + 1) * SUB].reshape(SUB * 128, 128)
        prod = jnp.dot(stream(block), wide, preferred_element_type=F32)
        part = jnp.sum(prod.reshape(SUB, 128, RANK) * b[None], axis=1)
        out[n * SUB : (n + 1) * SUB, :] = part[:, 0:128]
        out[128 + n * SUB : 128 + (n + 1) * SUB, :] = part[:, 128:256]


def sum_over_x(copies, held, wide, a, turned, acc):
    acc[...] = jnp.zeros((128, RANK), F32)
    for n in range(ROWS // SUB):
        if n * SUB % (ROWS // CHUNKS) == 0:
            copies[n * SUB // (ROWS // CHUNKS)].wait()
        block = held[n * SUB : (n + 1) * SUB]
        if turned:
            block = jnp.swapaxes(block, 1, 2)
        prod = jnp.dot(
            stream(block.reshape(SUB * 128, 128)), wide, preferred_element_type=F32
        ).reshape(SUB, 128, RANK)
        total = acc[...]
        for i in range(SUB):
            row = n * SUB + i
            total = total + prod[i] * a[row : row + 1, :]
        acc[...] = total


def second_kernel(inv, tensor, red1, fa, fc, new_a, out, held, acc, sems):
    copies = fetch(tensor, held, sems)
    mix = get_half(red1, 256) * get_half(red1, 640)
    a = updated(fa[...], get_mttkrp(red1), mix)
    new_a[...] = a
    put_gram(out, gram_of(a) * inv)
    sum_over_x(copies, held, weights(fc[...]), a, False, acc)
    put_mttkrp(out, acc[...])


def third_kernel(inv, tensor, red1, red2, fa, fb, new_b, out, held, acc, sems):
    copies = fetch(tensor, held, sems)
    mix = get_gram(red2) * get_half(red1, 640)
    b = updated(fb[...], get_mttkrp(red2), mix)
    new_b[...] = b
    put_gram(out, gram_of(b) * inv)
    sum_over_x(copies, held, weights(b), fa[...], True, acc)
    put_mttkrp(out, acc[...])


def fourth_kernel(red2, red3, fc, new_c):
    mix = get_gram(red2) * get_gram(red3)
    new_c[...] = updated(fc[...], get_mttkrp(red3), mix)


VMEM_SPEC = pl.BlockSpec(memory_space=pltpu.VMEM)
ANY_SPEC = pl.BlockSpec(memory_space=pl.ANY)
HELD = pltpu.VMEM((ROWS, 128, 128), F32)
ACC = pltpu.VMEM((128, RANK), F32)
SEMS = pltpu.SemaphoreType.DMA((CHUNKS,))
FACTOR = jax.ShapeDtypeStruct((128, RANK), F32)


def buffer(rows):
    return jax.ShapeDtypeStruct((rows, 128), F32)


def kernel_call(body, name, n_in, outs, scratch):
    return pl.pallas_call(
        body,
        out_shape=outs,
        in_specs=([ANY_SPEC] if scratch else []) + [VMEM_SPEC] * n_in,
        out_specs=jax.tree.map(lambda _: VMEM_SPEC, outs),
        scratch_shapes=scratch,
        compiler_params=pltpu.CompilerParams(vmem_limit_bytes=56 * 2**20),
        name=name,
    )


def all_reduce(buf, axes, n):
    parts = buf.reshape(n, buf.shape[0] // n, 128)
    got = lax.all_to_all(parts, axes, 0, 0, tiled=True)
    mine = jnp.sum(got, axis=0)
    full = lax.all_to_all(jnp.broadcast_to(mine, parts.shape), axes, 0, 0, tiled=True)
    return full.reshape(buf.shape)


def per_device(sizes, tensor, factor_a, factor_b, factor_c):
    px, py, mz = sizes
    buf1 = kernel_call(
        functools.partial(first_kernel, 1.0 / mz, 1.0 / py), "mttkrp_a", 2, buffer(1024), [HELD, SEMS]
    )(tensor, factor_b, factor_c)
    red1 = all_reduce(buf1, ("py", "mz"), py * mz)
    new_a, buf2 = kernel_call(
        functools.partial(second_kernel, 1.0 / mz), "mttkrp_b", 3, [FACTOR, buffer(768)], [HELD, ACC, SEMS]
    )(tensor, red1, factor_a, factor_c)
    red2 = all_reduce(buf2, ("px", "mz"), px * mz)
    new_b, buf3 = kernel_call(
        functools.partial(third_kernel, 1.0 / px), "mttkrp_c", 4, [FACTOR, buffer(768)], [HELD, ACC, SEMS]
    )(tensor, red1, red2, new_a, factor_b)
    red3 = all_reduce(buf3, ("px", "py"), px * py)
    new_c = kernel_call(fourth_kernel, "update_c", 3, FACTOR, [])(red2, red3, factor_c)
    return (new_a, new_b, new_c)


def solution(mesh):
    sizes = tuple(mesh.shape[a] for a in ("px", "py", "mz"))
    in_specs = (P("px", "py", "mz"), P("px", None), P("py", None), P("mz", None))
    out_specs = (P("px", None), P("py", None), P("mz", None))
    return jax.shard_map(
        functools.partial(per_device, sizes),
        mesh=mesh,
        in_specs=in_specs,
        out_specs=out_specs,
        check_vma=False,
    )
```

time: 1210 us -> 165 us (0.14)
  waiting for transfers between devices: 1030 us -> 0 us
  blocking collectives: 0 us -> 122 us
  matrix products: 115 us -> 0 us
  Pallas kernels: 0 us -> 41.9 us
  local copies, waits for them, and re-layouts: 34 us -> 0.09 us
  between operations: 14.5 us -> 0.69 us
    psum x7 -> x0, waiting for transfers between devices: 1030 us -> none  [the longest x1 493 us: per_device(): mttkrp_a = lax.psum(local_a, ('py', 'mz'))]
    all_to_all x0 -> x6, blocking collectives: none -> 122 us  [the longest x3 67.7 us: all_reduce(): got = lax.all_to_all(parts, axes, 0, 0, tiled=True)]
    dot_general x14 -> x0, matrix products: 115 us -> none  [the longest x1 40.3 us: per_device(): jnp.einsum('rjk,kr->jr', partial_a, factor_c, precision=exact_mode, prefe...]
    pallas_call x0 -> x4, Pallas kernels: none -> 41.9 us  [the longest x1 13.4 us: per_device(): kernel_call(functools.partial(third_kernel, 1.0 / px), 'mttkrp_c', 4, [FA...]
    unnamed x20 -> x0, local copies, waits for them, and re-layouts: 24.3 us -> none
  transfers between devices with their start and end apart: 7 -> 0, of which waited for: 6 -> 0; matrix products, arithmetic and copies ran while one was open for 11% -> 0% of each run, Pallas kernels for 0% -> 0%
where the time goes in v1:
time: 165 us; the launch traced here: 164 us
  blocking collectives  122 us (74%)
  Pallas kernels  41.9 us (25%)
    all_to_all x3, blocking collectives, all_reduce(): got = lax.all_to_all(parts, axes, 0, 0, tiled=True)  67.7 us
    all_to_all x3, blocking collectives, all_reduce(): lax.all_to_all(jnp.broadcast_to(mine, parts.shape), axes, 0, 0, tiled=True)  53.8 us
    pallas_call x1, Pallas kernels, per_device(): kernel_call(functools.partial(third_kernel, 1.0 / px), 'mttkrp_c', 4, [FA...  13.4 us
    pallas_call x1, Pallas kernels, per_device(): kernel_call(functools.partial(first_kernel, 1.0 / mz, 1.0 / py), 'mttkrp_...  13 us
    pallas_call x1, Pallas kernels, per_device(): kernel_call(functools.partial(second_kernel, 1.0 / mz), 'mttkrp_b', 3, [F...  13 us

profile of v1, /device:TPU:1, one launch (start us, length us, event | category | flops | bytes accessed | tf_op | source)
XLA Modules:
  0.0 164.4 jit_solution(1332925490725888048)
XLA Ops:
  0.6 13.0 %mttkrp_a.1 = f32[1024,128]{1,0:T(8,128)} custom-call(f32[128,128,128]{2,1,0:T(8,128)} %tensor.5, f32[128,256]{1,0:T(8,128)} %fb.3, f32[128,256]{1,0:T(8,128)} %fc.5), custom_call_target="tpu_custom_call" | custom-call | tf_op jit(solution)/shard_map/mttkrp_a/pallas_call | solution.py:184
  13.7 22.8 %all_to_all.30 = f32[64,16,128]{2,1,0:T(8,128)S(1)} all-to-all(f32[64,16,128]{2,1,0:T(8,128)} %bitcast.10), channel_id=1, replica_groups=mesh['px'=4,'py'=8,'mz'=8] {'py','mz'}, dimensions={0} | all-to-all | bytes 1048576 | tf_op jit(solution)/shard_map/all_to_all | solution.py:176
  36.4 0.1 reduce_sum.27
  36.5 16.8 %all_to_all.31 = f32[64,16,128]{2,1,0:T(8,128)} all-to-all(f32[64,16,128]{2,1,0:T(8,128)S(1)} %broadcast_in_dim.9), channel_id=1, replica_groups=mesh['px'=4,'py'=8,'mz'=8] {'py','mz'}, dimensions={0} | all-to-all | bytes 1048576 | tf_op jit(solution)/shard_map/all_to_all | solution.py:178
  53.3 13.0 %mttkrp_b.1 = (f32[128,256]{1,0:T(8,128)}, f32[768,128]{1,0:T(8,128)}) custom-call(f32[128,128,128]{2,1,0:T(8,128)} %tensor.5, f32[1024,128]{1,0:T(8,128)} %bitcast.6, f32[128,256]{1,0:T(8,128)} %fa.1, f32[128,256]{1,0:T(8,128)} %fc.5), custom_call_target="tpu_custom_call" | custom-call | tf_op jit(solution)/shard_map/mttkrp_b/pallas_call | solution.py:188
  66.3 22.2 %all_to_all.32 = f32[32,24,128]{2,1,0:T(8,128)S(1)} all-to-all(f32[32,24,128]{2,1,0:T(8,128)} %bitcast.13), channel_id=1, replica_groups=mesh['px'=4,'py'=8,'mz'=8] {'px','mz'}, dimensions={0} | all-to-all | bytes 786432 | tf_op jit(solution)/shard_map/all_to_all | solution.py:176
  88.5 17.8 %all_to_all.33 = f32[32,24,128]{2,1,0:T(8,128)} all-to-all(f32[32,24,128]{2,1,0:T(8,128)S(1)} %broadcast_in_dim.10), channel_id=1, replica_groups=mesh['px'=4,'py'=8,'mz'=8] {'px','mz'}, dimensions={0} | all-to-all | bytes 786432 | tf_op jit(solution)/shard_map/all_to_all | solution.py:178
  106.4 13.4 %mttkrp_c.1 = (f32[128,256]{1,0:T(8,128)}, f32[768,128]{1,0:T(8,128)}) custom-call(f32[128,128,128]{2,1,0:T(8,128)} %tensor.5, f32[1024,128]{1,0:T(8,128)} %bitcast.7, f32[768,128]{1,0:T(8,128)} %bitcast.8, f32[128,256]{1,0:T(8,128)} %get-tuple-element.4.fa, f32[128,256]{1,0:T(8,128)} %fb.3), custom_call_target="tpu_custom_call" | custom-call | tf_op jit(solution)/shard_map/mttkrp_c/pallas_call | solution.py:192
  119.8 22.8 %all_to_all.34 = f32[32,24,128]{2,1,0:T(8,128)S(1)} all-to-all(f32[32,24,128]{2,1,0:T(8,128)} %bitcast.12), channel_id=1, replica_groups=mesh['px'=4,'py'=8,'mz'=8] {'px','py'}, dimensions={0} | all-to-all | bytes 786432 | tf_op jit(solution)/shard_map/all_to_all | solution.py:176
  142.7 19.2 %all_to_all.35 = f32[32,24,128]{2,1,0:T(8,128)} all-to-all(f32[32,24,128]{2,1,0:T(8,128)S(1)} %broadcast_in_dim.11), channel_id=1, replica_groups=mesh['px'=4,'py'=8,'mz'=8] {'px','py'}, dimensions={0} | all-to-all | bytes 786432 | tf_op jit(solution)/shard_map/all_to_all | solution.py:178
  161.9 2.5 %update_c.1 = f32[128,256]{1,0:T(8,128)} custom-call(f32[768,128]{1,0:T(8,128)} %bitcast.9, f32[768,128]{1,0:T(8,128)} %bitcast.11, f32[128,256]{1,0:T(8,128)} %fc.5), custom_call_target="tpu_custom_call" | custom-call | tf_op jit(solution)/shard_map/update_c/pallas_call | solution.py:196
  (5 shorter events, 0.2 us)

commit v2 on v1

--- a/solution.py
+++ b/solution.py
@@ -13,7 +13,7 @@
 EXACT = lax.Precision.HIGHEST
 ROWS = 128
 RANK = 256
-CHUNKS = 8
+CHUNKS = 4
 SUB = 16
 
 
@@ -33,15 +33,20 @@
 
 
 def gram_of(factor):
+    hi, lo = split(factor)
     return lax.dot_general(
-        factor, factor, (((0,), (0,)), ((), ())), precision=EXACT, preferred_element_type=F32
+        jnp.concatenate([hi, lo, hi], axis=0),
+        jnp.concatenate([hi, hi, lo], axis=0),
+        (((0,), (0,)), ((), ())),
+        preferred_element_type=F32,
     )
 
 
 def updated(factor, mttkrp, mix):
     scale = jnp.sum(mix, axis=0, keepdims=True) + 1.0
+    wide = weights(mix)
     for _ in range(PASSES):
-        product = jnp.dot(factor, mix, precision=EXACT, preferred_element_type=F32)
+        product = jnp.dot(stream(factor), wide, preferred_element_type=F32)
         factor = jnp.maximum(factor + (mttkrp - product) / scale, 0.0)
     return factor
 
@@ -83,8 +88,8 @@
     for c in range(CHUNKS):
         part = pl.ds(c * step, step)
         copies.append(pltpu.make_async_copy(tensor.at[part], held.at[part], sems.at[c]))
-    for copy in copies:
-        copy.start()
+    copies[0].start()
+    copies[1].start()
     return copies
 
 
@@ -96,7 +101,10 @@
     wide = weights(c)
     for n in range(ROWS // SUB):
         if n * SUB % (ROWS // CHUNKS) == 0:
-            copies[n * SUB // (ROWS // CHUNKS)].wait()
+            at = n * SUB // (ROWS // CHUNKS)
+            copies[at].wait()
+            if at + 2 < CHUNKS:
+                copies[at + 2].start()
         block = held[n * SUB : (n + 1) * SUB].reshape(SUB * 128, 128)
         prod = jnp.dot(stream(block), wide, preferred_element_type=F32)
         part = jnp.sum(prod.reshape(SUB, 128, RANK) * b[None], axis=1)
@@ -108,7 +116,10 @@
     acc[...] = jnp.zeros((128, RANK), F32)
     for n in range(ROWS // SUB):
         if n * SUB % (ROWS // CHUNKS) == 0:
-            copies[n * SUB // (ROWS // CHUNKS)].wait()
+            at = n * SUB // (ROWS // CHUNKS)
+            copies[at].wait()
+            if at + 2 < CHUNKS:
+                copies[at + 2].start()
         block = held[n * SUB : (n + 1) * SUB]
         if turned:
             block = jnp.swapaxes(block, 1, 2)
@@ -148,7 +159,7 @@
 
 
 VMEM_SPEC = pl.BlockSpec(memory_space=pltpu.VMEM)
-ANY_SPEC = pl.BlockSpec(memory_space=pl.ANY)
+ANY_SPEC = pl.BlockSpec(memory_space=pltpu.HBM)
 HELD = pltpu.VMEM((ROWS, 128, 128), F32)
 ACC = pltpu.VMEM((128, RANK), F32)
 SEMS = pltpu.SemaphoreType.DMA((CHUNKS,))
@@ -166,7 +177,7 @@
         in_specs=([ANY_SPEC] if scratch else []) + [VMEM_SPEC] * n_in,
         out_specs=jax.tree.map(lambda _: VMEM_SPEC, outs),
         scratch_shapes=scratch,
-        compiler_params=pltpu.CompilerParams(vmem_limit_bytes=56 * 2**20),
+        compiler_params=pltpu.CompilerParams(vmem_limit_bytes=48 * 2**20),
         name=name,
     )
 

time: 165 us -> 148 us (0.90)
  Pallas kernels: 41.9 us -> 22.7 us
  local copies, waits for them, and re-layouts: 0.09 us -> 2.81 us
    pallas_call x1, Pallas kernels: 13 us -> 6.79 us  [per_device(): kernel_call(functools.partial(first_kernel, 1.0 / mz, 1.0 / py), 'mttkrp_...]
    pallas_call x1, Pallas kernels: 13 us -> 7.17 us  [per_device(): kernel_call(functools.partial(second_kernel, 1.0 / mz), 'mttkrp_b', 3, [F...]
    pallas_call x1, Pallas kernels: 13.4 us -> 7.67 us  [per_device(): kernel_call(functools.partial(third_kernel, 1.0 / px), 'mttkrp_c', 4, [FA...]
    unnamed x0 -> x12, local copies, waits for them, and re-layouts: none -> 2.72 us
where the time goes in v2:
time: 148 us; the launch traced here: 147 us
  blocking collectives  121 us (82%)
  Pallas kernels  22.7 us (15%)
  local copies, waits for them, and re-layouts  2.81 us (2%)
    all_to_all x3, blocking collectives, all_reduce(): got = lax.all_to_all(parts, axes, 0, 0, tiled=True)  67 us
    all_to_all x3, blocking collectives, all_reduce(): lax.all_to_all(jnp.broadcast_to(mine, parts.shape), axes, 0, 0, tiled=True)  53.8 us
    pallas_call x1, Pallas kernels, per_device(): kernel_call(functools.partial(third_kernel, 1.0 / px), 'mttkrp_c', 4, [FA...  7.67 us
    pallas_call x1, Pallas kernels, per_device(): kernel_call(functools.partial(second_kernel, 1.0 / mz), 'mttkrp_b', 3, [F...  7.17 us
    pallas_call x1, Pallas kernels, per_device(): kernel_call(functools.partial(first_kernel, 1.0 / mz, 1.0 / py), 'mttkrp_...  6.79 us

profile of v2, /device:TPU:1, one launch (start us, length us, event | category | flops | bytes accessed | tf_op | source)
XLA Modules:
  0.0 147.2 jit_solution(13111340628835620179)
XLA Ops:
  0.6 0.0 copy-start
  0.6 0.9 copy-done
  1.5 0.0 copy-start.2
  1.5 0.9 copy-done.2
  2.4 0.0 copy-start.1
  2.4 0.0 copy-start.4
  2.4 6.8 %mttkrp_a.1 = f32[1024,128]{1,0:T(8,128)S(1)} custom-call(f32[128,128,128]{2,1,0:T(8,128)} %tensor.5, f32[128,256]{1,0:T(8,128)S(1)} %copy-done.2, f32[128,256]{1,0:T(8,128)S(1)} %copy-done), custom_call_target="tpu_custom_call" | custom-call | tf_op jit(solution)/shard_map/mttkrp_a/pallas_call | solution.py:195
  9.2 0.0 copy-start.3
  9.3 22.7 %all_to_all.30 = f32[64,16,128]{2,1,0:T(8,128)S(1)} all-to-all(f32[64,16,128]{2,1,0:T(8,128)S(1)} %bitcast.10), channel_id=1, replica_groups=mesh['px'=4,'py'=8,'mz'=8] {'py','mz'}, dimensions={0} | all-to-all | bytes 1048576 | tf_op jit(solution)/shard_map/all_to_all | solution.py:187
  31.9 0.1 reduce_sum.27
  32.0 16.7 %all_to_all.31 = f32[64,16,128]{2,1,0:T(8,128)S(1)} all-to-all(f32[64,16,128]{2,1,0:T(8,128)S(1)} %broadcast_in_dim.9), channel_id=1, replica_groups=mesh['px'=4,'py'=8,'mz'=8] {'py','mz'}, dimensions={0} | all-to-all | bytes 1048576 | tf_op jit(solution)/shard_map/all_to_all | solution.py:189
  48.7 0.0 copy-done.1
  48.7 0.0 copy-done.4
  48.7 7.2 %mttkrp_b.1 = (f32[128,256]{1,0:T(8,128)}, f32[768,128]{1,0:T(8,128)S(1)}) custom-call(f32[128,128,128]{2,1,0:T(8,128)} %tensor.5, f32[1024,128]{1,0:T(8,128)S(1)} %bitcast.6, f32[128,256]{1,0:T(8,128)S(1)} %copy-done.4, f32[128,256]{1,0:T(8,128)S(1)} %copy-done.1), custom_call_target="tpu_custom_call" | custom-call | tf_op jit(solution)/shard_map/mttkrp_b/pallas_call | solution.py:199
  55.9 22.0 %all_to_all.32 = f32[32,24,128]{2,1,0:T(8,128)S(1)} all-to-all(f32[32,24,128]{2,1,0:T(8,128)S(1)} %bitcast.13), channel_id=1, replica_groups=mesh['px'=4,'py'=8,'mz'=8] {'px','mz'}, dimensions={0} | all-to-all | bytes 786432 | tf_op jit(solution)/shard_map/all_to_all | solution.py:187
  77.9 17.7 %all_to_all.33 = f32[32,24,128]{2,1,0:T(8,128)S(1)} all-to-all(f32[32,24,128]{2,1,0:T(8,128)S(1)} %broadcast_in_dim.10), channel_id=1, replica_groups=mesh['px'=4,'py'=8,'mz'=8] {'px','mz'}, dimensions={0} | all-to-all | bytes 786432 | tf_op jit(solution)/shard_map/all_to_all | solution.py:189
  95.7 0.0 copy-done.3
  95.7 0.0 copy-start.5
  95.7 0.9 copy-done.5
  96.6 7.7 %mttkrp_c.1 = (f32[128,256]{1,0:T(8,128)}, f32[768,128]{1,0:T(8,128)S(1)}) custom-call(f32[128,128,128]{2,1,0:T(8,128)} %tensor.5, f32[1024,128]{1,0:T(8,128)S(1)} %bitcast.7, f32[768,128]{1,0:T(8,128)S(1)} %bitcast.8, f32[128,256]{1,0:T(8,128)S(1)} %copy-done.5, f32[128,256]{1,0:T(8,128)S(1)} %copy-done.3), custom_call_target="tpu_custom_call" | custom-call | tf_op jit(solution)/shard_map/mttkrp_c/pallas_call | solution.py:203
  104.2 22.4 %all_to_all.34 = f32[32,24,128]{2,1,0:T(8,128)S(1)} all-to-all(f32[32,24,128]{2,1,0:T(8,128)S(1)} %bitcast.12), channel_id=1, replica_groups=mesh['px'=4,'py'=8,'mz'=8] {'px','py'}, dimensions={0} | all-to-all | bytes 786432 | tf_op jit(solution)/shard_map/all_to_all | solution.py:187
  126.7 19.4 %all_to_all.35 = f32[32,24,128]{2,1,0:T(8,128)S(1)} all-to-all(f32[32,24,128]{2,1,0:T(8,128)S(1)} %broadcast_in_dim.11), channel_id=1, replica_groups=mesh['px'=4,'py'=8,'mz'=8] {'px','py'}, dimensions={0} | all-to-all | bytes 786432 | tf_op jit(solution)/shard_map/all_to_all | solution.py:189
  146.1 1.1 update_c.1
  (5 shorter events, 0.2 us)
Async XLA Ops:
  0.6 0.9 copy-start
  1.5 0.9 copy-start.2
  2.4 46.3 %copy-start.1 = (f32[128,256]{1,0:T(8,128)S(1)}, f32[128,256]{1,0:T(8,128)}, u32[]{:S(2)}) copy-start(f32[128,256]{1,0:T(8,128)} %fc.5) | copy-start | bytes 393220
  2.4 46.3 %copy-start.4 = (f32[128,256]{1,0:T(8,128)S(1)}, f32[128,256]{1,0:T(8,128)}, u32[]{:S(2)}) copy-start(f32[128,256]{1,0:T(8,128)} %fa.1) | copy-start | bytes 393220
  9.2 86.4 %copy-start.3 = (f32[128,256]{1,0:T(8,128)S(1)}, f32[128,256]{1,0:T(8,128)}, u32[]{:S(2)}) copy-start(f32[128,256]{1,0:T(8,128)} %fb.3) | copy-start | bytes 393220
  95.7 0.9 copy-start.5

commit v3 on v2

--- a/solution.py
+++ b/solution.py
@@ -5,6 +5,7 @@
 from jax import lax
 from jax.experimental import pallas as pl
 from jax.experimental.pallas import tpu as pltpu
+from jax.sharding import Mesh
 from jax.sharding import PartitionSpec as P
 
 PASSES = 2
@@ -60,26 +61,38 @@
     return jnp.concatenate([buf[0:128, :], buf[128:256, :]], axis=1)
 
 
-def put_half(buf, at, gram):
-    buf[at : at + 128, :] = gram[0:128, 0:128]
-    buf[at + 128 : at + 256, :] = gram[0:128, 128:256]
-    buf[at + 256 : at + 384, :] = gram[128:256, 128:256]
-
-
-def get_half(buf, at):
-    corner = buf[at + 128 : at + 256, :]
-    top = jnp.concatenate([buf[at : at + 128, :], corner], axis=1)
-    low = jnp.concatenate([corner.T, buf[at + 256 : at + 384, :]], axis=1)
+def put_half(out, core, at, gram):
+    out[core, at : at + 128, :] = gram[0:128, 0:128]
+    out[core, at + 128 : at + 192, :] = gram[0:64, 128:256]
+    out[1 - core, at : at + 64, :] = gram[64:128, 128:256]
+    out[1 - core, at + 64 : at + 192, :] = gram[128:256, 128:256]
+
+
+def halves(a, b):
+    first = lax.axis_index("core") == 0
+    return jnp.where(first, a, b), jnp.where(first, b, a)
+
+
+def get_rows(lo, hi):
+    left = jnp.concatenate([lo[0:64], hi[0:64]], axis=0)
+    right = jnp.concatenate([lo[64:128], hi[64:128]], axis=0)
+    return jnp.concatenate([left, right], axis=1)
+
+
+def get_half(lo, hi, at):
+    corner = jnp.concatenate([lo[at + 128 : at + 192], hi[at : at + 64]], axis=0)
+    top = jnp.concatenate([lo[at : at + 128], corner], axis=1)
+    low = jnp.concatenate([corner.T, hi[at + 64 : at + 192]], axis=1)
     return jnp.concatenate([top, low], axis=0)
 
 
 def put_gram(buf, gram):
-    buf[256:512, :] = gram[:, 0:128]
-    buf[512:768, :] = gram[:, 128:256]
-
-
-def get_gram(buf):
-    return jnp.concatenate([buf[256:512, :], buf[512:768, :]], axis=1)
+    first = lax.axis_index("core") == 0
+    buf[256:512, :] = jnp.where(first, gram[:, 0:128], gram[:, 128:256])
+
+
+def get_gram(mine, other):
+    return jnp.concatenate(halves(mine[256:512, :], other[...]), axis=1)
 
 
 def fetch(tensor, held, sems):
@@ -96,8 +109,9 @@
 def first_kernel(inv_b, inv_c, tensor, fb, fc, out, held, sems):
     copies = fetch(tensor, held, sems)
     b, c = fb[...], fc[...]
-    put_half(out, 256, gram_of(b) * inv_b)
-    put_half(out, 640, gram_of(c) * inv_c)
+    core = lax.axis_index("core")
+    put_half(out, core, 128, gram_of(b) * inv_b)
+    put_half(out, core, 320, gram_of(c) * inv_c)
     wide = weights(c)
     for n in range(ROWS // SUB):
         if n * SUB % (ROWS // CHUNKS) == 0:
@@ -108,8 +122,10 @@
         block = held[n * SUB : (n + 1) * SUB].reshape(SUB * 128, 128)
         prod = jnp.dot(stream(block), wide, preferred_element_type=F32)
         part = jnp.sum(prod.reshape(SUB, 128, RANK) * b[None], axis=1)
-        out[n * SUB : (n + 1) * SUB, :] = part[:, 0:128]
-        out[128 + n * SUB : 128 + (n + 1) * SUB, :] = part[:, 128:256]
+        half, at = divmod(n * SUB, 64)
+        slot = core if half == 0 else 1 - core
+        out[slot, at : at + SUB, :] = part[:, 0:128]
+        out[slot, 64 + at : 64 + at + SUB, :] = part[:, 128:256]
 
 
 def sum_over_x(copies, held, wide, a, turned, acc):
@@ -133,29 +149,36 @@
         acc[...] = total
 
 
-def second_kernel(inv, tensor, red1, fa, fc, new_a, out, held, acc, sems):
+def second_kernel(inv, tensor, mine1, other1, fa, fc, new_a, again, out, held, acc, sems):
     copies = fetch(tensor, held, sems)
-    mix = get_half(red1, 256) * get_half(red1, 640)
-    a = updated(fa[...], get_mttkrp(red1), mix)
+    lo, hi = halves(mine1[...], other1[...])
+    mix = get_half(lo, hi, 128) * get_half(lo, hi, 320)
+    a = updated(fa[...], get_rows(lo, hi), mix)
     new_a[...] = a
+    again[...] = a
     put_gram(out, gram_of(a) * inv)
     sum_over_x(copies, held, weights(fc[...]), a, False, acc)
     put_mttkrp(out, acc[...])
 
 
-def third_kernel(inv, tensor, red1, red2, fa, fb, new_b, out, held, acc, sems):
+def third_kernel(inv, tensor, mine1, other1, red2, swap2, fa, fb, new_b, out, held, acc, sems):
     copies = fetch(tensor, held, sems)
-    mix = get_gram(red2) * get_half(red1, 640)
+    mix = get_gram(red2, swap2) * get_half(*halves(mine1[...], other1[...]), 320)
     b = updated(fb[...], get_mttkrp(red2), mix)
     new_b[...] = b
-    put_gram(out, gram_of(b) * inv)
+    core = lax.axis_index("core")
+    put_half(out, core, 128, gram_of(b) * inv)
     sum_over_x(copies, held, weights(b), fa[...], True, acc)
-    put_mttkrp(out, acc[...])
-
-
-def fourth_kernel(red2, red3, fc, new_c):
-    mix = get_gram(red2) * get_gram(red3)
-    new_c[...] = updated(fc[...], get_mttkrp(red3), mix)
+    for half, slot in enumerate((core, 1 - core)):
+        part = acc[half * 64 : half * 64 + 64, :]
+        out[slot, 0:64, :] = part[:, 0:128]
+        out[slot, 64:128, :] = part[:, 128:256]
+
+
+def fourth_kernel(red2, swap2, mine3, other3, fc, new_c):
+    lo, hi = halves(mine3[...], other3[...])
+    mix = get_gram(red2, swap2) * get_half(lo, hi, 128)
+    new_c[...] = updated(fc[...], get_rows(lo, hi), mix)
 
 
 VMEM_SPEC = pl.BlockSpec(memory_space=pltpu.VMEM)
@@ -190,32 +213,48 @@
     return full.reshape(buf.shape)
 
 
+def swap(x):
+    return lax.ppermute(x, "core", [(0, 1), (1, 0)])
+
+
+def core_first(buf, axes, n):
+    mine = all_reduce(buf[0] + swap(buf[1]), axes, n)
+    return mine, swap(mine)
+
+
+def pair(rows):
+    return jax.ShapeDtypeStruct((2, rows, 128), F32)
+
+
 def per_device(sizes, tensor, factor_a, factor_b, factor_c):
-    px, py, mz = sizes
+    px, y, core, mz = sizes
     buf1 = kernel_call(
-        functools.partial(first_kernel, 1.0 / mz, 1.0 / py), "mttkrp_a", 2, buffer(1024), [HELD, SEMS]
+        functools.partial(first_kernel, 1.0 / mz, 1.0 / (y * core)), "mttkrp_a", 2, pair(512), [HELD, SEMS]
     )(tensor, factor_b, factor_c)
-    red1 = all_reduce(buf1, ("py", "mz"), py * mz)
-    new_a, buf2 = kernel_call(
-        functools.partial(second_kernel, 1.0 / mz), "mttkrp_b", 3, [FACTOR, buffer(768)], [HELD, ACC, SEMS]
-    )(tensor, red1, factor_a, factor_c)
+    mine1, other1 = core_first(buf1, ("y", "mz"), y * mz)
+    new_a, held_a, buf2 = kernel_call(
+        functools.partial(second_kernel, 1.0 / mz), "mttkrp_b", 4, [FACTOR, FACTOR, buffer(512)], [HELD, ACC, SEMS]
+    )(tensor, mine1, other1, factor_a, factor_c)
     red2 = all_reduce(buf2, ("px", "mz"), px * mz)
+    swap2 = swap(red2[256:512])
     new_b, buf3 = kernel_call(
-        functools.partial(third_kernel, 1.0 / px), "mttkrp_c", 4, [FACTOR, buffer(768)], [HELD, ACC, SEMS]
-    )(tensor, red1, red2, new_a, factor_b)
-    red3 = all_reduce(buf3, ("px", "py"), px * py)
-    new_c = kernel_call(fourth_kernel, "update_c", 3, FACTOR, [])(red2, red3, factor_c)
+        functools.partial(third_kernel, 1.0 / px), "mttkrp_c", 6, [FACTOR, pair(320)], [HELD, ACC, SEMS]
+    )(tensor, mine1, other1, red2, swap2, held_a, factor_b)
+    mine3, other3 = core_first(buf3, ("px", "y"), px * y)
+    new_c = kernel_call(fourth_kernel, "update_c", 5, FACTOR, [])(red2, swap2, mine3, other3, factor_c)
     return (new_a, new_b, new_c)
 
 
 def solution(mesh):
-    sizes = tuple(mesh.shape[a] for a in ("px", "py", "mz"))
-    in_specs = (P("px", "py", "mz"), P("px", None), P("py", None), P("mz", None))
-    out_specs = (P("px", None), P("py", None), P("mz", None))
+    px, py, mz = (mesh.shape[a] for a in ("px", "py", "mz"))
+    sizes = (px, py // 2, 2, mz)
+    fine = Mesh(mesh.devices.reshape(sizes), ("px", "y", "core", "mz"))
+    by_y = P(("y", "core"), None)
+    in_specs = (P("px", ("y", "core"), "mz"), P("px", None), by_y, P("mz", None))
     return jax.shard_map(
         functools.partial(per_device, sizes),
-        mesh=mesh,
+        mesh=fine,
         in_specs=in_specs,
-        out_specs=out_specs,
+        out_specs=(P("px", None), by_y, P("mz", None)),
         check_vma=False,
     )

time: 148 us -> 132 us (0.89)
  blocking collectives: 121 us -> 88.8 us
  starting transfers between devices: 0 us -> 12.5 us
  waiting for transfers between devices: 0 us -> 5.37 us
    all_to_all x3, blocking collectives: 67 us -> 47.3 us  [all_reduce(): got = lax.all_to_all(parts, axes, 0, 0, tiled=True)]
    ppermute x0 -> x5, starting transfers between devices: none -> 12.5 us  [swap(): return lax.ppermute(x, 'core', [(0, 1), (1, 0)])]
    all_to_all x3, blocking collectives: 53.8 us -> 41.5 us  [all_reduce(): lax.all_to_all(jnp.broadcast_to(mine, parts.shape), axes, 0, 0, tiled=True)]
    ppermute x0 -> x5, waiting for transfers between devices: none -> 5.37 us  [swap(): return lax.ppermute(x, 'core', [(0, 1), (1, 0)])]
  transfers between devices with their start and end apart: 0 -> 5, of which waited for: 0 -> 5; matrix products, arithmetic and copies ran while one was open for 0% -> 0% of each run, Pallas kernels for 0% -> 0%
where the time goes in v3:
time: 132 us
  blocking collectives  88.8 us (67%)
  Pallas kernels  22.4 us (17%)
  starting transfers between devices  12.5 us (9%)
  waiting for transfers between devices  5.37 us (4%)
  local copies, waits for them, and re-layouts  1.94 us (1%)
    all_to_all x3, blocking collectives, all_reduce(): got = lax.all_to_all(parts, axes, 0, 0, tiled=True)  47.3 us
    all_to_all x3, blocking collectives, all_reduce(): lax.all_to_all(jnp.broadcast_to(mine, parts.shape), axes, 0, 0, tiled=True)  41.5 us
    ppermute x5, starting transfers between devices, swap(): return lax.ppermute(x, 'core', [(0, 1), (1, 0)])  12.5 us
    pallas_call x1, Pallas kernels, per_device(): kernel_call(functools.partial(third_kernel, 1.0 / px), 'mttkrp_c', 6, [FA...  7.32 us
    pallas_call x1, Pallas kernels, per_device(): kernel_call(functools.partial(second_kernel, 1.0 / mz), 'mttkrp_b', 4, [F...  7.17 us
    pallas_call x1, Pallas kernels, per_device(): kernel_call(functools.partial(first_kernel, 1.0 / mz, 1.0 / (y * core)),...  6.76 us
    ppermute x5, waiting for transfers between devices, swap(): return lax.ppermute(x, 'core', [(0, 1), (1, 0)])  5.37 us
  transfers between devices with their start and end apart: 5, of which 5 were waited for; matrix products, arithmetic and copies ran while one was open for 0% of the time, Pallas kernels for 0%

profile of v3, /device:TPU:1, one launch (start us, length us, event | category | flops | bytes accessed | tf_op | source)
XLA Modules:
  0.0 131.9 jit_solution(1128617253527428220)
XLA Ops:
  0.6 0.0 copy-start
  0.6 0.9 copy-done
  1.5 0.0 copy-start.2
  1.5 0.9 copy-done.2
  2.4 0.0 copy-start.1
  2.4 0.0 copy-start.4
  2.4 6.8 %mttkrp_a.1 = f32[2,512,128]{2,1,0:T(8,128)S(1)} custom-call(f32[128,128,128]{2,1,0:T(8,128)} %tensor.5, f32[128,256]{1,0:T(8,128)S(1)} %copy-done.2, f32[128,256]{1,0:T(8,128)S(1)} %copy-done), custom_call_target="tpu_custom_call" | custom-call | tf_op jit(solution)/shard_map/mttkrp_a/pallas_call | solution.py:231
  9.2 0.0 copy-start.3
  9.3 3.3 %collective-permute-start = (f32[512,128]{1,0:T(8,128)S(1)}, f32[512,128]{1,0:T(8,128)S(1)}, u32[]{:S(2)}, u32[]{:S(2)}) collective-permute-start(f32[512,128]{1,0:T(8,128)S(1)} %slice_bitcast_fusion), channel_id=1, source_target_pairs={{0,8},{8,0},{1,9},{9,1},{2,10},{10,2},{3,11},{11,3},{4,12},{12,4},... | collective-permute-start | bytes 786440 | tf_op jit(solution)/shard_map/ppermute | solution.py:217
  12.6 1.2 collective-permute-done
  13.8 14.5 %all_to_all.30 = f32[32,16,128]{2,1,0:T(8,128)S(1)} all-to-all(f32[32,16,128]{2,1,0:T(8,128)S(1)} %bitcast.21), channel_id=1, replica_groups=mesh['px'=4,'y'=4,'core'=2,'mz'=8] {'y','mz'}, dimensions={0} | all-to-all | bytes 524288 | tf_op jit(solution)/shard_map/all_to_all | solution.py:210
  28.3 12.7 %all_to_all.31 = f32[32,16,128]{2,1,0:T(8,128)S(1)} all-to-all(f32[32,16,128]{2,1,0:T(8,128)S(1)} %broadcast_in_dim.9), channel_id=1, replica_groups=mesh['px'=4,'y'=4,'core'=2,'mz'=8] {'y','mz'}, dimensions={0} | all-to-all | bytes 524288 | tf_op jit(solution)/shard_map/all_to_all | solution.py:212
  41.0 2.3 %collective-permute-start.1 = (f32[512,128]{1,0:T(8,128)S(1)}, f32[512,128]{1,0:T(8,128)S(1)}, u32[]{:S(2)}, u32[]{:S(2)}) collective-permute-start(f32[512,128]{1,0:T(8,128)S(1)} %bitcast.17), channel_id=1, source_target_pairs={{0,8},{8,0},{1,9},{9,1},{2,10},{10,2},{3,11},{11,3},{4,12},{12,4},... | collective-permute-start | bytes 786440 | tf_op jit(solution)/shard_map/ppermute | solution.py:217
  43.3 1.2 collective-permute-done.1.other1
  44.4 0.0 copy-done.1
  44.4 0.0 copy-done.4
  44.4 7.2 %mttkrp_b.1 = (f32[128,256]{1,0:T(8,128)}, f32[128,256]{1,0:T(8,128)S(1)}, f32[512,128]{1,0:T(8,128)S(1)}) custom-call(f32[128,128,128]{2,1,0:T(8,128)} %tensor.5, f32[512,128]{1,0:T(8,128)S(1)} %bitcast.18, f32[512,128]{1,0:T(8,128)S(1)} %collective-permute-done.1.other1, f32[128,256]{1,0:T(8,128)S(1)} %copy-done.4, f32[128,256]{1,0:T(8,128)S(1)} %copy-done.1), custom_call_target="tpu_custom_call" | custom-call | tf_op jit(solution)/shard_map/mttkrp_b/pallas_call | solution.py:235
  51.6 19.9 %all_to_all.32 = f32[32,16,128]{2,1,0:T(8,128)S(1)} all-to-all(f32[32,16,128]{2,1,0:T(8,128)S(1)} %bitcast.20), channel_id=1, replica_groups=mesh['px'=4,'y'=4,'core'=2,'mz'=8] {'px','mz'}, dimensions={0} | all-to-all | bytes 524288 | tf_op jit(solution)/shard_map/all_to_all | solution.py:210
  71.6 15.0 %all_to_all.33 = f32[32,16,128]{2,1,0:T(8,128)S(1)} all-to-all(f32[32,16,128]{2,1,0:T(8,128)S(1)} %broadcast_in_dim.10), channel_id=1, replica_groups=mesh['px'=4,'y'=4,'core'=2,'mz'=8] {'px','mz'}, dimensions={0} | all-to-all | bytes 524288 | tf_op jit(solution)/shard_map/all_to_all | solution.py:212
  86.7 3.6 %collective-permute-start.2 = (f32[256,128]{1,0:T(8,128)S(1)}, f32[256,128]{1,0:T(8,128)S(1)}, u32[]{:S(2)}, u32[]{:S(2)}) collective-permute-start(f32[256,128]{1,0:T(8,128)S(1)} %bitcast.22), channel_id=1, source_target_pairs={{0,8},{8,0},{1,9},{9,1},{2,10},{10,2},{3,11},{11,3},{4,12},{12,4},... | collective-permute-start | bytes 393224 | tf_op jit(solution)/shard_map/ppermute | solution.py:217
  90.3 1.0 collective-permute-done.2.swap2
  91.2 0.0 copy-done.3
  91.2 7.3 %mttkrp_c.1 = (f32[128,256]{1,0:T(8,128)}, f32[2,320,128]{2,1,0:T(8,128)S(1)}) custom-call(f32[128,128,128]{2,1,0:T(8,128)} %tensor.5, f32[512,128]{1,0:T(8,128)S(1)} %bitcast.19, f32[512,128]{1,0:T(8,128)S(1)} %collective-permute-done.1.other1, f32[512,128]{1,0:T(8,128)S(1)} %bitcast.15, f32[256,128]{1,0:T(8,128)S(1)} %collective-permute-done.2.swap2, ...), custom_call_target="tpu_custom_call" | custom-call | tf_op jit(solution)/shard_map/mttkrp_c/pallas_call | solution.py:240
  98.6 0.4 collective-permute-start.3
  99.0 1.0 collective-permute-done.3
  100.1 12.9 %all_to_all.34 = f32[16,20,128]{2,1,0:T(8,128)S(1)} all-to-all(f32[16,20,128]{2,1,0:T(8,128)S(1)} %reshape.29), channel_id=1, replica_groups=mesh['px'=4,'y'=4,'core'=2,'mz'=8] {'px','y'}, dimensions={0} | all-to-all | bytes 327680 | tf_op jit(solution)/shard_map/all_to_all | solution.py:210
  113.0 13.8 %all_to_all.35 = f32[16,20,128]{2,1,0:T(8,128)S(1)} all-to-all(f32[16,20,128]{2,1,0:T(8,128)S(1)} %broadcast_in_dim.11), channel_id=1, replica_groups=mesh['px'=4,'y'=4,'core'=2,'mz'=8] {'px','y'}, dimensions={0} | all-to-all | bytes 327680 | tf_op jit(solution)/shard_map/all_to_all | solution.py:212
  126.9 2.9 %collective-permute-start.4 = (f32[320,128]{1,0:T(8,128)S(1)}, f32[320,128]{1,0:T(8,128)S(1)}, u32[]{:S(2)}, u32[]{:S(2)}) collective-permute-start(f32[320,128]{1,0:T(8,128)S(1)} %reshape.30.mine3), channel_id=1, source_target_pairs={{0,8},{8,0},{1,9},{9,1},{2,10},{10,2},{3,11},{11,3},{4,12},{12,4},... | collective-permute-start | bytes 491528 | tf_op jit(solution)/shard_map/ppermute | solution.py:217
  129.7 1.0 collective-permute-done.4.other3
  130.8 1.2 update_c.1
  (13 shorter events, 0.3 us)
Async XLA Ops:
  0.6 0.9 copy-start
  1.5 0.9 copy-start.2
  2.4 42.0 %copy-start.1 = (f32[128,256]{1,0:T(8,128)S(1)}, f32[128,256]{1,0:T(8,128)}, u32[]{:S(2)}) copy-start(f32[128,256]{1,0:T(8,128)} %fc.5) | copy-start | bytes 393220
  2.4 42.0 %copy-start.4 = (f32[128,256]{1,0:T(8,128)S(1)}, f32[128,256]{1,0:T(8,128)}, u32[]{:S(2)}) copy-start(f32[128,256]{1,0:T(8,128)} %fa.1) | copy-start | bytes 393220
  9.2 82.0 %copy-start.3 = (f32[128,256]{1,0:T(8,128)S(1)}, f32[128,256]{1,0:T(8,128)}, u32[]{:S(2)}) copy-start(f32[128,256]{1,0:T(8,128)} %fb.3) | copy-start | bytes 393220
  9.3 4.5 %collective-permute-start = (f32[512,128]{1,0:T(8,128)S(1)}, f32[512,128]{1,0:T(8,128)S(1)}, u32[]{:S(2)}, u32[]{:S(2)}) collective-permute-start(f32[512,128]{1,0:T(8,128)S(1)} %slice_bitcast_fusion), channel_id=1, source_target_pairs={{0,8},{8,0},{1,9},{9,1},{2,10},{10,2},{3,11},{11,3},{4,12},{12,4},... | collective-permute-start | bytes 786440 | tf_op jit(solution)/shard_map/ppermute | solution.py:217
  41.0 3.5 %collective-permute-start.1 = (f32[512,128]{1,0:T(8,128)S(1)}, f32[512,128]{1,0:T(8,128)S(1)}, u32[]{:S(2)}, u32[]{:S(2)}) collective-permute-start(f32[512,128]{1,0:T(8,128)S(1)} %bitcast.17), channel_id=1, source_target_pairs={{0,8},{8,0},{1,9},{9,1},{2,10},{10,2},{3,11},{11,3},{4,12},{12,4},... | collective-permute-start | bytes 786440 | tf_op jit(solution)/shard_map/ppermute | solution.py:217
  86.7 4.6 %collective-permute-start.2 = (f32[256,128]{1,0:T(8,128)S(1)}, f32[256,128]{1,0:T(8,128)S(1)}, u32[]{:S(2)}, u32[]{:S(2)}) collective-permute-start(f32[256,128]{1,0:T(8,128)S(1)} %bitcast.22), channel_id=1, source_target_pairs={{0,8},{8,0},{1,9},{9,1},{2,10},{10,2},{3,11},{11,3},{4,12},{12,4},... | collective-permute-start | bytes 393224 | tf_op jit(solution)/shard_map/ppermute | solution.py:217
  98.6 1.5 %collective-permute-start.3 = (f32[320,128]{1,0:T(8,128)S(1)}, f32[320,128]{1,0:T(8,128)S(1)}, u32[]{:S(2)}, u32[]{:S(2)}) collective-permute-start(f32[320,128]{1,0:T(8,128)S(1)} %slice_bitcast_fusion.2), channel_id=1, source_target_pairs={{0,8},{8,0},{1,9},{9,1},{2,10},{10,2},{3,11},{11,3},{4,12},{12,4},... | collective-permute-start | bytes 491528 | tf_op jit(solution)/shard_map/ppermute | solution.py:217
  126.9 3.9 %collective-permute-start.4 = (f32[320,128]{1,0:T(8,128)S(1)}, f32[320,128]{1,0:T(8,128)S(1)}, u32[]{:S(2)}, u32[]{:S(2)}) collective-permute-start(f32[320,128]{1,0:T(8,128)S(1)} %reshape.30.mine3), channel_id=1, source_target_pairs={{0,8},{8,0},{1,9},{9,1},{2,10},{10,2},{3,11},{11,3},{4,12},{12,4},... | collective-permute-start | bytes 491528 | tf_op jit(solution)/shard_map/ppermute | solution.py:217

commit v4 on v3

--- a/solution.py
+++ b/solution.py
@@ -88,11 +88,13 @@
 
 def put_gram(buf, gram):
     first = lax.axis_index("core") == 0
-    buf[256:512, :] = jnp.where(first, gram[:, 0:128], gram[:, 128:256])
+    lo = jnp.concatenate([gram[0:128, 0:128], gram[0:64, 128:256]], axis=0)
+    hi = jnp.concatenate([gram[64:128, 128:256], gram[128:256, 128:256]], axis=0)
+    buf[256:448, :] = jnp.where(first, lo, hi)
 
 
 def get_gram(mine, other):
-    return jnp.concatenate(halves(mine[256:512, :], other[...]), axis=1)
+    return get_half(*halves(mine[256:448, :], other[...]), 0)
 
 
 def fetch(tensor, held, sems):
@@ -106,9 +108,9 @@
     return copies
 
 
-def first_kernel(inv_b, inv_c, tensor, fb, fc, out, held, sems):
+def first_kernel(inv_b, inv_c, tensor, fbc, out, held, sems):
     copies = fetch(tensor, held, sems)
-    b, c = fb[...], fc[...]
+    b, c = fbc[0], fbc[1]
     core = lax.axis_index("core")
     put_half(out, core, 128, gram_of(b) * inv_b)
     put_half(out, core, 320, gram_of(c) * inv_c)
@@ -229,14 +231,14 @@
 def per_device(sizes, tensor, factor_a, factor_b, factor_c):
     px, y, core, mz = sizes
     buf1 = kernel_call(
-        functools.partial(first_kernel, 1.0 / mz, 1.0 / (y * core)), "mttkrp_a", 2, pair(512), [HELD, SEMS]
-    )(tensor, factor_b, factor_c)
+        functools.partial(first_kernel, 1.0 / mz, 1.0 / (y * core)), "mttkrp_a", 1, pair(512), [HELD, SEMS]
+    )(tensor, jnp.stack([factor_b, factor_c]))
     mine1, other1 = core_first(buf1, ("y", "mz"), y * mz)
     new_a, held_a, buf2 = kernel_call(
-        functools.partial(second_kernel, 1.0 / mz), "mttkrp_b", 4, [FACTOR, FACTOR, buffer(512)], [HELD, ACC, SEMS]
+        functools.partial(second_kernel, 1.0 / mz), "mttkrp_b", 4, [FACTOR, FACTOR, buffer(448)], [HELD, ACC, SEMS]
     )(tensor, mine1, other1, factor_a, factor_c)
     red2 = all_reduce(buf2, ("px", "mz"), px * mz)
-    swap2 = swap(red2[256:512])
+    swap2 = swap(red2[256:448])
     new_b, buf3 = kernel_call(
         functools.partial(third_kernel, 1.0 / px), "mttkrp_c", 6, [FACTOR, pair(320)], [HELD, ACC, SEMS]
     )(tensor, mine1, other1, red2, swap2, held_a, factor_b)

time: 132 us -> 132 us (level)
  local copies, waits for them, and re-layouts: 1.94 us -> 0.18 us
    unnamed x10 -> x6, local copies, waits for them, and re-layouts: 1.81 us -> 0.01 us
where the time goes in v4:
time: 132 us; the launch traced here: 131 us
  blocking collectives  88.8 us (67%)
  Pallas kernels  22.4 us (17%)
  starting transfers between devices  12.5 us (9%)
  waiting for transfers between devices  5.35 us (4%)
    all_to_all x3, blocking collectives, all_reduce(): got = lax.all_to_all(parts, axes, 0, 0, tiled=True)  47.3 us
    all_to_all x3, blocking collectives, all_reduce(): lax.all_to_all(jnp.broadcast_to(mine, parts.shape), axes, 0, 0, tiled=True)  41.5 us
    ppermute x5, starting transfers between devices, swap(): return lax.ppermute(x, 'core', [(0, 1), (1, 0)])  12.5 us
    pallas_call x1, Pallas kernels, per_device(): kernel_call(functools.partial(third_kernel, 1.0 / px), 'mttkrp_c', 6, [FA...  7.36 us
    pallas_call x1, Pallas kernels, per_device(): kernel_call(functools.partial(second_kernel, 1.0 / mz), 'mttkrp_b', 4, [F...  7.16 us
    pallas_call x1, Pallas kernels, per_device(): kernel_call(functools.partial(first_kernel, 1.0 / mz, 1.0 / (y * core)),...  6.73 us
    ppermute x5, waiting for transfers between devices, swap(): return lax.ppermute(x, 'core', [(0, 1), (1, 0)])  5.35 us
  transfers between devices with their start and end apart: 5, of which 5 were waited for; matrix products, arithmetic and copies ran while one was open for 0% of the time, Pallas kernels for 0%

profile of v4, /device:TPU:1, one launch (start us, length us, event | category | flops | bytes accessed | tf_op | source)
XLA Modules:
  0.0 131.2 jit_solution(14219429313666194754)
XLA Ops:
  0.6 0.0 copy-start
  0.6 0.0 copy-start.2
  0.7 1.0 pad_maximum_fusion.fbc
  1.7 6.7 %mttkrp_a.1 = f32[2,512,128]{2,1,0:T(8,128)S(1)} custom-call(f32[128,128,128]{2,1,0:T(8,128)} %tensor.5, f32[2,128,256]{2,1,0:T(8,128)S(1)} %pad_maximum_fusion.fbc), custom_call_target="tpu_custom_call" | custom-call | tf_op jit(solution)/shard_map/mttkrp_a/pallas_call | solution.py:233
  8.4 0.0 copy-start.1
  8.5 3.3 %collective-permute-start = (f32[512,128]{1,0:T(8,128)S(1)}, f32[512,128]{1,0:T(8,128)S(1)}, u32[]{:S(2)}, u32[]{:S(2)}) collective-permute-start(f32[512,128]{1,0:T(8,128)S(1)} %slice_bitcast_fusion), channel_id=1, source_target_pairs={{0,8},{8,0},{1,9},{9,1},{2,10},{10,2},{3,11},{11,3},{4,12},{12,4},... | collective-permute-start | bytes 786440 | tf_op jit(solution)/shard_map/ppermute | solution.py:219
  11.8 1.2 collective-permute-done
  13.0 14.5 %all_to_all.30 = f32[32,16,128]{2,1,0:T(8,128)S(1)} all-to-all(f32[32,16,128]{2,1,0:T(8,128)S(1)} %bitcast.19), channel_id=1, replica_groups=mesh['px'=4,'y'=4,'core'=2,'mz'=8] {'y','mz'}, dimensions={0} | all-to-all | bytes 524288 | tf_op jit(solution)/shard_map/all_to_all | solution.py:212
  27.5 12.7 %all_to_all.31 = f32[32,16,128]{2,1,0:T(8,128)S(1)} all-to-all(f32[32,16,128]{2,1,0:T(8,128)S(1)} %broadcast_in_dim.9), channel_id=1, replica_groups=mesh['px'=4,'y'=4,'core'=2,'mz'=8] {'y','mz'}, dimensions={0} | all-to-all | bytes 524288 | tf_op jit(solution)/shard_map/all_to_all | solution.py:214
  40.2 2.3 %collective-permute-start.1 = (f32[512,128]{1,0:T(8,128)S(1)}, f32[512,128]{1,0:T(8,128)S(1)}, u32[]{:S(2)}, u32[]{:S(2)}) collective-permute-start(f32[512,128]{1,0:T(8,128)S(1)} %bitcast.14), channel_id=1, source_target_pairs={{0,8},{8,0},{1,9},{9,1},{2,10},{10,2},{3,11},{11,3},{4,12},{12,4},... | collective-permute-start | bytes 786440 | tf_op jit(solution)/shard_map/ppermute | solution.py:219
  42.5 1.2 collective-permute-done.1.other1
  43.6 0.0 copy-done
  43.6 0.0 copy-done.2
  43.6 7.2 %mttkrp_b.1 = (f32[128,256]{1,0:T(8,128)}, f32[128,256]{1,0:T(8,128)S(1)}, f32[448,128]{1,0:T(8,128)S(1)}) custom-call(f32[128,128,128]{2,1,0:T(8,128)} %tensor.5, f32[512,128]{1,0:T(8,128)S(1)} %bitcast.15, f32[512,128]{1,0:T(8,128)S(1)} %collective-permute-done.1.other1, f32[128,256]{1,0:T(8,128)S(1)} %copy-done.2, f32[128,256]{1,0:T(8,128)S(1)} %copy-done), custom_call_target="tpu_custom_call" | custom-call | tf_op jit(solution)/shard_map/mttkrp_b/pallas_call | solution.py:237
  50.8 20.0 %all_to_all.32 = f32[32,14,128]{2,1,0:T(8,128)S(1)} all-to-all(f32[32,14,128]{2,1,0:T(8,128)S(1)} %reshape.26), channel_id=1, replica_groups=mesh['px'=4,'y'=4,'core'=2,'mz'=8] {'px','mz'}, dimensions={0} | all-to-all | bytes 458752 | tf_op jit(solution)/shard_map/all_to_all | solution.py:212
  70.9 15.0 %all_to_all.33 = f32[32,14,128]{2,1,0:T(8,128)S(1)} all-to-all(f32[32,14,128]{2,1,0:T(8,128)S(1)} %broadcast_in_dim.10), channel_id=1, replica_groups=mesh['px'=4,'y'=4,'core'=2,'mz'=8] {'px','mz'}, dimensions={0} | all-to-all | bytes 458752 | tf_op jit(solution)/shard_map/all_to_all | solution.py:214
  85.9 3.6 %collective-permute-start.2 = (f32[192,128]{1,0:T(8,128)S(1)}, f32[192,128]{1,0:T(8,128)S(1)}, u32[]{:S(2)}, u32[]{:S(2)}) collective-permute-start(f32[192,128]{1,0:T(8,128)S(1)} %slice.22), channel_id=1, source_target_pairs={{0,8},{8,0},{1,9},{9,1},{2,10},{10,2},{3,11},{11,3},{4,12},{12,4},... | collective-permute-start | bytes 294920 | tf_op jit(solution)/shard_map/ppermute | solution.py:219
  89.5 0.9 collective-permute-done.2.swap2
  90.5 0.0 copy-done.1
  90.5 7.4 %mttkrp_c.1 = (f32[128,256]{1,0:T(8,128)}, f32[2,320,128]{2,1,0:T(8,128)S(1)}) custom-call(f32[128,128,128]{2,1,0:T(8,128)} %tensor.5, f32[512,128]{1,0:T(8,128)S(1)} %bitcast.16, f32[512,128]{1,0:T(8,128)S(1)} %collective-permute-done.1.other1, f32[448,128]{1,0:T(8,128)S(1)} %reshape.27.red2, f32[192,128]{1,0:T(8,128)S(1)} %collective-permute-done.2.swap2, ...), custom_call_target="tpu_custom_call" | custom-call | tf_op jit(solution)/shard_map/mttkrp_c/pallas_call | solution.py:242
  97.8 0.4 collective-permute-start.3
  98.3 1.0 collective-permute-done.3
  99.4 12.9 %all_to_all.34 = f32[16,20,128]{2,1,0:T(8,128)S(1)} all-to-all(f32[16,20,128]{2,1,0:T(8,128)S(1)} %reshape.28), channel_id=1, replica_groups=mesh['px'=4,'y'=4,'core'=2,'mz'=8] {'px','y'}, dimensions={0} | all-to-all | bytes 327680 | tf_op jit(solution)/shard_map/all_to_all | solution.py:212
  112.3 13.8 %all_to_all.35 = f32[16,20,128]{2,1,0:T(8,128)S(1)} all-to-all(f32[16,20,128]{2,1,0:T(8,128)S(1)} %broadcast_in_dim.11), channel_id=1, replica_groups=mesh['px'=4,'y'=4,'core'=2,'mz'=8] {'px','y'}, dimensions={0} | all-to-all | bytes 327680 | tf_op jit(solution)/shard_map/all_to_all | solution.py:214
  126.1 2.9 %collective-permute-start.4 = (f32[320,128]{1,0:T(8,128)S(1)}, f32[320,128]{1,0:T(8,128)S(1)}, u32[]{:S(2)}, u32[]{:S(2)}) collective-permute-start(f32[320,128]{1,0:T(8,128)S(1)} %reshape.29.mine3), channel_id=1, source_target_pairs={{0,8},{8,0},{1,9},{9,1},{2,10},{10,2},{3,11},{11,3},{4,12},{12,4},... | collective-permute-start | bytes 491528 | tf_op jit(solution)/shard_map/ppermute | solution.py:219
  129.0 1.0 collective-permute-done.4.other3
  130.0 1.2 update_c.1
  (15 shorter events, 0.3 us)
Async XLA Ops:
  0.6 43.0 %copy-start = (f32[128,256]{1,0:T(8,128)S(1)}, f32[128,256]{1,0:T(8,128)}, u32[]{:S(2)}) copy-start(f32[128,256]{1,0:T(8,128)} %fc.3) | copy-start | bytes 393220
  0.6 43.0 %copy-start.2 = (f32[128,256]{1,0:T(8,128)S(1)}, f32[128,256]{1,0:T(8,128)}, u32[]{:S(2)}) copy-start(f32[128,256]{1,0:T(8,128)} %fa.1) | copy-start | bytes 393220
  8.4 82.0 %copy-start.1 = (f32[128,256]{1,0:T(8,128)S(1)}, f32[128,256]{1,0:T(8,128)}, u32[]{:S(2)}) copy-start(f32[128,256]{1,0:T(8,128)} %fb.1) | copy-start | bytes 393220
  8.5 4.5 %collective-permute-start = (f32[512,128]{1,0:T(8,128)S(1)}, f32[512,128]{1,0:T(8,128)S(1)}, u32[]{:S(2)}, u32[]{:S(2)}) collective-permute-start(f32[512,128]{1,0:T(8,128)S(1)} %slice_bitcast_fusion), channel_id=1, source_target_pairs={{0,8},{8,0},{1,9},{9,1},{2,10},{10,2},{3,11},{11,3},{4,12},{12,4},... | collective-permute-start | bytes 786440 | tf_op jit(solution)/shard_map/ppermute | solution.py:219
  40.2 3.5 %collective-permute-start.1 = (f32[512,128]{1,0:T(8,128)S(1)}, f32[512,128]{1,0:T(8,128)S(1)}, u32[]{:S(2)}, u32[]{:S(2)}) collective-permute-start(f32[512,128]{1,0:T(8,128)S(1)} %bitcast.14), channel_id=1, source_target_pairs={{0,8},{8,0},{1,9},{9,1},{2,10},{10,2},{3,11},{11,3},{4,12},{12,4},... | collective-permute-start | bytes 786440 | tf_op jit(solution)/shard_map/ppermute | solution.py:219
  85.9 4.5 %collective-permute-start.2 = (f32[192,128]{1,0:T(8,128)S(1)}, f32[192,128]{1,0:T(8,128)S(1)}, u32[]{:S(2)}, u32[]{:S(2)}) collective-permute-start(f32[192,128]{1,0:T(8,128)S(1)} %slice.22), channel_id=1, source_target_pairs={{0,8},{8,0},{1,9},{9,1},{2,10},{10,2},{3,11},{11,3},{4,12},{12,4},... | collective-permute-start | bytes 294920 | tf_op jit(solution)/shard_map/ppermute | solution.py:219
  97.8 1.5 %collective-permute-start.3 = (f32[320,128]{1,0:T(8,128)S(1)}, f32[320,128]{1,0:T(8,128)S(1)}, u32[]{:S(2)}, u32[]{:S(2)}) collective-permute-start(f32[320,128]{1,0:T(8,128)S(1)} %slice_bitcast_fusion.2), channel_id=1, source_target_pairs={{0,8},{8,0},{1,9},{9,1},{2,10},{10,2},{3,11},{11,3},{4,12},{12,4},... | collective-permute-start | bytes 491528 | tf_op jit(solution)/shard_map/ppermute | solution.py:219
  126.1 3.9 %collective-permute-start.4 = (f32[320,128]{1,0:T(8,128)S(1)}, f32[320,128]{1,0:T(8,128)S(1)}, u32[]{:S(2)}, u32[]{:S(2)}) collective-permute-start(f32[320,128]{1,0:T(8,128)S(1)} %reshape.29.mine3), channel_id=1, source_target_pairs={{0,8},{8,0},{1,9},{9,1},{2,10},{10,2},{3,11},{11,3},{4,12},{12,4},... | collective-permute-start | bytes 491528 | tf_op jit(solution)/shard_map/ppermute | solution.py:219
